TPU v7x, 256 devices: a whole 4x4x8 slice. The times are simulated.
256 devices in a mesh: dp: 4 (over x), fsdp: 64 (over z, y, core).
Axes of the slice: x: 4, y: 4, z: 8, core: 2. Of those that a mesh axis runs over, the one named last changes fastest.
Arguments:
- inputs: bfloat16 [512, 16384], P('dp', 'fsdp'), may hold values from -140 to 140
- norm_gain_vector: bfloat16 [16384], P('fsdp'), may hold values from 0.5 to 1.5
- weight: bfloat16 [16384, 16384], P(None, 'fsdp'), may hold values from -0.046875 to 0.046875
- down_adapters: bfloat16 [16384, 16, 32], P('fsdp'), may hold values from -0.046875 to 0.046875
- up_adapters: bfloat16 [16, 32, 16384], P(None, None, 'fsdp'), may hold values from -1 to 1
- tenant: int32 [512], P('dp'), may hold values from 0 to 15
- tenant_slot_index: int32 [16], replicated, may hold values from 0 to 31, as said below
- live_row_count: int32 [4], P('dp'), may hold values from 1 to 128, 320 in all
- cotangent: bfloat16 [512, 16384], P('dp', 'fsdp'), may hold values from -6 to 6
- down_row_factor: float32 [32, 16384], P('dp', 'fsdp'), may hold values from 300 to 30000
- down_column_factor: float32 [32, 32], P('dp'), may hold values from 300 to 30000
- up_row_factor: float32 [32, 32], P('dp'), may hold values from 0.5 to 50
- up_column_factor: float32 [32, 16384], P('dp', 'fsdp'), may hold values from 0.5 to 50
Outputs:
- projected: bfloat16 [512, 16384], P('dp', 'fsdp')
- normed_gradient_transposed: bfloat16 [16384, 512], P('fsdp', 'dp')
- update_a: float32 [32, 16384, 32], P('dp', 'fsdp')
- update_b: float32 [32, 32, 16384], P('dp', None, 'fsdp')
- row_a_new: float32 [32, 16384], P('dp', 'fsdp')
- col_a_new: float32 [32, 32], P('dp')
- row_b_new: float32 [32, 32], P('dp')
- col_b_new: float32 [32, 16384], P('dp', 'fsdp')
Inputs may be any that keep to these rules, and one draw needn't show every extreme that they name: Distinct slots; tenant t's optimizer state is in slot tenant_slot_index[t], owned by data group tenant_slot_index[t] // 8; every group owns at most 8 tenants and some group owns exactly 8. The first live_row_count[g] rows of data group g are live; some group has all 128 live; the counts sum to 320.
All inputs are finite; a program needn't handle non-finite values.
Results may differ from a plain program's by a relative error of at most 0.0095.
Values may be sent and summed in bfloat16 or wider, within the bound.
No kernel may reach another device: no remote copies, remote signals or barrier semaphores. Data moves between devices by JAX's collectives and lax.ppermute only.
A program may use at most 128 MiB of HBM per device.

v0:
```python
import jax
import jax.numpy as jnp
from jax import lax
from jax.sharding import PartitionSpec as P

ADAPTER_SCALE = 0.5
BETA_TWO = 0.9
SQ_EPS = 1e-30
RMS_EPS = 1e-05


def gather_turned(arrays, axis, dims):
    turned = [jnp.moveaxis(a, dim, 0) for a, dim in zip(arrays, dims)]
    widths = [t[0].size for t in turned]
    both = jnp.concatenate([t.reshape(-1, w) for t, w in zip(turned, widths)], axis=1)
    filled = lax.all_gather(both, axis, axis=0, tiled=True)
    pieces = jnp.split(filled, [sum(widths[:k]) for k in range(1, len(widths))], axis=1)
    return tuple(
        (
            jnp.moveaxis(b.reshape(-1, *t.shape[1:]), 0, dim)
            for b, t, dim in zip(pieces, turned, dims)
        )
    )


def copy_for_each(value, axis):
    copies = jnp.broadcast_to(value, (lax.axis_size(axis), *value.shape))
    return lax.all_to_all(copies, axis, split_axis=0, concat_axis=0, tiled=True)


def of_everyone(value, axis):
    return copy_for_each(value, axis).sum(axis=0)


def over_copies(value, axis):
    return copy_for_each(value, axis).astype(jnp.float32).sum(axis=0)


def together(arrays, axis):
    vector, at, done = (jnp.concatenate([a.reshape(-1) for a in arrays]), 0, [])
    subtotal = of_everyone(vector, axis)
    for a in arrays:
        done.append(subtotal[at : at + a.size].reshape(a.shape))
        at += a.size
    return tuple(done)


def on_device(
    inputs,
    norm_gain_vector,
    weight,
    down_adapters,
    up_adapters,
    tenant,
    tenant_slot_index,
    live_row_count,
    cotangent,
    down_row_factor,
    down_column_factor,
    up_row_factor,
    up_column_factor,
):
    highest_precision = lax.Precision.HIGHEST
    rows, shard_local_width = inputs.shape
    full_width = weight.shape[0]
    tenant_index = down_adapters.shape[1]
    device_rank = down_adapters.shape[2]
    lane = lax.axis_index("fsdp")
    contract_last = (((1,), (1,)), ((), ()))
    contract_first = (((0,), (0,)), ((), ()))
    whole_x, whole_gain = gather_turned((inputs, norm_gain_vector), "fsdp", (1, 0))
    whole_f = whole_x.astype(jnp.float32)
    power = jnp.sum(whole_f * whole_f, axis=1, keepdims=True)
    scale = lax.rsqrt(power / full_width + RMS_EPS)
    normed_full = (whole_f * scale * whole_gain.astype(jnp.float32)).astype(jnp.bfloat16)
    frozen_output = jnp.dot(normed_full, weight, preferred_element_type=jnp.float32)
    normalized_input = lax.dynamic_slice_in_dim(
        normed_full, lane * shard_local_width, shard_local_width, 1
    )
    pick = tenant[:, None] == lax.iota(jnp.int32, tenant_index)[None, :]
    pick_b = pick.astype(jnp.bfloat16)
    pick_f = pick.astype(jnp.float32)
    down_flattened = down_adapters.reshape(shard_local_width, tenant_index * device_rank)
    up_flattened = up_adapters.reshape(tenant_index * device_rank, up_adapters.shape[2])
    inner_all = jnp.dot(normalized_input, down_flattened, preferred_element_type=jnp.float32)
    inner_part = jnp.sum(
        inner_all.reshape(rows, tenant_index, device_rank) * pick_f[:, :, None], axis=1
    )
    inner = of_everyone(inner_part, "fsdp")
    spread_rows = (inner.astype(jnp.bfloat16)[:, None, :] * pick_b[:, :, None]).reshape(
        rows, tenant_index * device_rank
    )
    adapted_output = jnp.dot(spread_rows, up_flattened, preferred_element_type=jnp.float32)
    projected = (frozen_output + ADAPTER_SCALE * adapted_output).astype(jnp.bfloat16)
    live = lax.iota(jnp.int32, rows) < live_row_count[0]
    output_gradient = jnp.where(live[:, None], cotangent, jnp.zeros_like(cotangent))
    back_all = lax.dot_general(
        output_gradient, up_flattened, contract_last, preferred_element_type=jnp.float32
    )
    back_part = jnp.sum(
        back_all.reshape(rows, tenant_index, device_rank) * pick_f[:, :, None], axis=1
    )
    back = of_everyone(back_part, "fsdp")
    backward_spread_rows = (back.astype(jnp.bfloat16)[:, None, :] * pick_b[:, :, None]).reshape(
        rows, tenant_index * device_rank
    )
    frozen_input_gradient = lax.psum_scatter(
        lax.dot_general(weight, output_gradient, contract_last, preferred_element_type=jnp.float32),
        "fsdp",
        scatter_dimension=0,
        tiled=True,
    )
    adapter_input_gradient = lax.dot_general(
        down_flattened, backward_spread_rows, contract_last, preferred_element_type=jnp.float32
    )
    normed_gradient_transposed = (
        frozen_input_gradient + ADAPTER_SCALE * adapter_input_gradient
    ).astype(jnp.bfloat16)
    down_gradient = (
        ADAPTER_SCALE
        * lax.dot_general(
            normalized_input,
            backward_spread_rows,
            contract_first,
            preferred_element_type=jnp.float32,
        )
    ).reshape(shard_local_width, tenant_index, device_rank)
    up_gradient = (
        ADAPTER_SCALE
        * lax.dot_general(
            spread_rows, output_gradient, contract_first, preferred_element_type=jnp.float32
        )
    ).reshape(tenant_index, device_rank, output_gradient.shape[1])
    owned = down_row_factor.shape[0]
    summed_a, summed_b = (
        over_copies(down_gradient.astype(jnp.bfloat16), "dp").astype(jnp.float32),
        over_copies(up_gradient.astype(jnp.bfloat16), "dp").astype(jnp.float32),
    )
    mine = lax.iota(jnp.int32, owned) + lax.axis_index("dp") * owned
    owner_routing = (tenant_slot_index[None, :] == mine[:, None]).astype(jnp.float32)
    ga = jnp.einsum("st,ftr->sfr", owner_routing, summed_a, precision=highest_precision)
    gb = jnp.einsum("ho,oxk->hxk", owner_routing, summed_b, precision=highest_precision)
    sq_a = ga * ga + SQ_EPS
    sq_b = gb * gb + SQ_EPS
    row_a_new = BETA_TWO * down_row_factor + (1.0 - BETA_TWO) * (
        jnp.sum(sq_a, axis=2) / device_rank
    )
    col_b_new = BETA_TWO * up_column_factor + (1.0 - BETA_TWO) * (
        jnp.sum(sq_b, axis=1) / device_rank
    )
    col_sum, rowb_sum, meana_sum = together(
        (jnp.sum(sq_a, axis=1), jnp.sum(sq_b, axis=2), jnp.sum(row_a_new, axis=1)), "fsdp"
    )
    col_a_new = BETA_TWO * down_column_factor + (1.0 - BETA_TWO) * (col_sum / full_width)
    row_b_new = BETA_TWO * up_row_factor + (1.0 - BETA_TWO) * (rowb_sum / full_width)
    mean_a = meana_sum / full_width
    mean_b = jnp.sum(row_b_new, axis=1) / device_rank
    update_a = ga * lax.rsqrt(row_a_new[:, :, None] * col_a_new[:, None, :] / mean_a[:, None, None])
    update_b = gb * lax.rsqrt(row_b_new[:, :, None] * col_b_new[:, None, :] / mean_b[:, None, None])
    return (
        projected,
        normed_gradient_transposed,
        update_a,
        update_b,
        row_a_new,
        col_a_new,
        row_b_new,
        col_b_new,
    )


def solution(mesh):
    return jax.shard_map(
        on_device,
        mesh=mesh,
        in_specs=(
            P("dp", "fsdp"),
            P("fsdp"),
            P(None, "fsdp"),
            P("fsdp", None, None),
            P(None, None, "fsdp"),
            P("dp"),
            P(),
            P("dp"),
            P("dp", "fsdp"),
            P("dp", "fsdp"),
            P("dp", None),
            P("dp", None),
            P("dp", "fsdp"),
        ),
        out_specs=(
            P("dp", "fsdp"),
            P("fsdp", "dp"),
            P("dp", "fsdp", None),
            P("dp", None, "fsdp"),
            P("dp", "fsdp"),
            P("dp", None),
            P("dp", None),
            P("dp", "fsdp"),
        ),
        check_vma=False,
    )
```

profile of v0, /device:TPU:6, one launch (start us, length us, event | category | flops | bytes accessed | tf_op | source)
XLA Modules:
  0.0 264.9 jit_solution(11799860212287939905)
XLA Ops:
  7.2 0.0 copy-start
  7.2 0.0 all-gather.2.cloned.1.call-start
  7.2 1.0 copy.77
  8.2 0.8 reshape.145
  9.0 0.7 pad_maximum_fusion
  9.7 0.0 all-gather.2.cloned.1.call-update
  9.7 0.0 reduce-scatter.2.cloned.1.call-start
  10.4 9.5 %convolution_bitcast_fusion = f32[16384,128]{0,1:T(8,128)} fusion(bf16[16384,256]{1,0:T(8,128)(2,1)} %param.15, bf16[128,256]{1,0:T(8,128)(2,1)} %param.21, pred[128]{0:T(512)(128)(4,1)S(1)} %iota_compare_fusion.1), kind=kOutput, calls=%fused_computation | convolution fusion | flops 1073774592 | bytes 16842880 | tf_op jit(solution)/shard_map/dot_general | solution.py:108
  19.9 0.0 reduce-scatter.2.cloned.1.call-update
  19.9 0.6 copy-done.14
  20.5 0.2 copy-done.3
  20.7 0.3 fusion.6
  21.0 1.1 broadcast_in_dim.23
  22.2 12.1 %all-to-all-start.1 = ((f32[64,128,32]{1,2,0:T(8,128)}), f32[64,128,32]{1,2,0:T(8,128)S(1)}, u32[]{:S(2)}, u32[]{:S(2)}) async-start(f32[64,128,32]{1,2,0:T(8,128)} %broadcast_in_dim.23), calls=%async_computation.2 | async-start | bytes 2097152 | tf_op jit(solution)/shard_map/all_to_all | solution.py:28
  34.3 67.1 %all-gather.2.cloned.1.call-done = bf16[16384,129]{1,0:T(8,128)(2,1)} async-done(((bf16[256,129]{1,0:T(8,128)(2,1)}), bf16[16384,129]{1,0:T(8,128)(2,1)}) %all-gather.2.cloned.1.call-update) | async-done | bytes 4227088 | tf_op jit(solution)/shard_map/all_gather | solution.py:16
  101.3 3.9 %fusion = f32[128]{0:T(128)S(1)} fusion(bf16[16384,129]{1,0:T(8,128)(2,1)} %all-gather.2.cloned.1.call-done), kind=kLoop, calls=%fused_computation.3 | loop fusion | flops 6291328 | bytes 4194816 | tf_op jit(solution)/shard_map/reduce_sum | solution.py:73
  105.3 2.9 %convert_reduce_fusion = f32[16384]{0:T(1024)S(1)} fusion(bf16[16384,129]{1,0:T(8,128)(2,1)} %all-gather.2.cloned.1.call-done), kind=kLoop, calls=%fused_computation.6 | loop fusion | flops 16384 | bytes 98304 | tf_op jit(solution)/shard_map/convert_element_type | solution.py:75
  108.2 6.9 %fusion.2 = bf16[16384,128]{1,0:T(8,128)(2,1)S(1)} fusion(f32[16384]{0:T(1024)S(1)} %convert_reduce_fusion, f32[128]{0:T(128)S(1)} %add_rsqrt_fusion, bf16[16384,129]{1,0:T(8,128)(2,1)S(1)} %copy-done.2), kind=kLoop, calls=%fused_computation.5 | loop fusion | flops 8388608 | bytes 8454656 | tf_op jit(solution)/shard_map/convert_element_type | solution.py:75
  115.1 2.0 copy-done.1
  117.1 0.2 fusion.5
  117.4 1.2 broadcast_in_dim.20
  118.5 6.6 %all-to-all-start = ((f32[64,128,32]{1,2,0:T(8,128)}), f32[64,128,32]{1,2,0:T(8,128)S(1)}, u32[]{:S(2)}, u32[]{:S(2)}) async-start(f32[64,128,32]{1,2,0:T(8,128)} %broadcast_in_dim.20), calls=%async_computation | async-start | bytes 2097152 | tf_op jit(solution)/shard_map/all_to_all | solution.py:28
  125.2 0.1 reduce_sum.130
  125.3 28.8 %all-to-all-done = f32[64,128,32]{1,2,0:T(8,128)S(1)} async-done(((f32[64,128,32]{1,2,0:T(8,128)}), f32[64,128,32]{1,2,0:T(8,128)S(1)}, u32[]{:S(2)}, u32[]{:S(2)}) %all-to-all-start) | async-done | bytes 1048608 | tf_op jit(solution)/shard_map/all_to_all | solution.py:28
  154.1 0.1 reduce_sum.128
  154.2 1.1 fusion.3
  155.3 0.1 copy.79
  155.4 1.2 broadcast_in_dim.24
  156.6 4.6 %all-to-all-start.2 = ((bf16[4,256,16,32]{1,3,2,0:T(8,128)(2,1)}), bf16[4,256,16,32]{1,3,2,0:T(8,128)(2,1)S(1)}, u32[]{:S(2)}, u32[]{:S(2)}) async-start(bf16[4,256,16,32]{1,3,2,0:T(8,128)(2,1)} %broadcast_in_dim.24), calls=%async_computation.3 | async-start | bytes 2097152 | tf_op jit(solution)/shard_map/all_to_all | solution.py:28
  161.2 0.3 fusion.4
  161.5 12.1 %all-to-all-done.2 = bf16[4,256,16,32]{1,3,2,0:T(8,128)(2,1)S(1)} async-done(((bf16[4,256,16,32]{1,3,2,0:T(8,128)(2,1)}), bf16[4,256,16,32]{1,3,2,0:T(8,128)(2,1)S(1)}, u32[]{:S(2)}, u32[]{:S(2)}) %all-to-all-start.2) | async-done | bytes 1048608 | tf_op jit(solution)/shard_map/all_to_all | solution.py:28
  173.6 1.2 broadcast_in_dim.25
  174.8 5.6 %all-to-all-start.3 = ((bf16[4,16,32,256]{3,2,1,0:T(8,128)(2,1)}), bf16[4,16,32,256]{3,2,1,0:T(8,128)(2,1)S(1)}, u32[]{:S(2)}, u32[]{:S(2)}) async-start(bf16[4,16,32,256]{3,2,1,0:T(8,128)(2,1)} %broadcast_in_dim.25), calls=%async_computation.4 | async-start | bytes 2097152 | tf_op jit(solution)/shard_map/all_to_all | solution.py:28
  180.3 0.2 convert_reduce_fusion.2
  180.5 0.7 fusion.19
  181.2 0.1 copy.81
  181.3 0.1 reshape.137
  181.4 10.4 %all-to-all-done.3 = bf16[4,16,32,256]{3,2,1,0:T(8,128)(2,1)S(1)} async-done(((bf16[4,16,32,256]{3,2,1,0:T(8,128)(2,1)}), bf16[4,16,32,256]{3,2,1,0:T(8,128)(2,1)S(1)}, u32[]{:S(2)}, u32[]{:S(2)}) %all-to-all-start.3) | async-done | bytes 1048608 | tf_op jit(solution)/shard_map/all_to_all | solution.py:28
  191.8 0.2 convert_reduce_fusion.1
  191.9 0.7 fusion.21
  192.6 0.1 copy.83
  192.7 0.1 reshape.138
  192.8 0.1 fusion.40
  192.9 0.0 copy-start.5
  192.9 0.8 broadcast_in_dim.26
  193.7 7.1 %all-to-all-start.4 = ((f32[64,1,520]{2,1,0:T(1,128)}), f32[64,1,520]{2,1,0:T(1,128)S(1)}, u32[]{:S(2)}, u32[]{:S(2)}) async-start(f32[64,1,520]{2,1,0:T(1,128)} %broadcast_in_dim.26), calls=%async_computation.5 | async-start | bytes 327680 | tf_op jit(solution)/shard_map/all_to_all | solution.py:28
  200.8 0.0 copy-start.11
  200.8 0.0 copy-start.12
  200.8 6.3 %fusion.41 = f32[128,256]{1,0:T(8,128)S(1)} fusion(bf16[16384,128]{1,0:T(8,128)(2,1)} %copy-done.1, bf16[16384,256]{1,0:T(8,128)(2,1)} %param.15), kind=kOutput, calls=%fused_computation.74 | convolution fusion | flops 1073741824 | bytes 12713984 | tf_op jit(solution)/shard_map/dot_general | solution.py:76
  207.1 0.9 fusion.13
  208.0 5.4 %all-to-all-done.4 = f32[64,1,520]{2,1,0:T(1,128)S(1)} async-done(((f32[64,1,520]{2,1,0:T(1,128)}), f32[64,1,520]{2,1,0:T(1,128)S(1)}, u32[]{:S(2)}, u32[]{:S(2)}) %all-to-all-start.4) | async-done | bytes 133152 | tf_op jit(solution)/shard_map/all_to_all | solution.py:28
  213.4 0.1 reduce_sum.137
  213.5 0.1 mul.211
  213.6 0.1 fusion.39
  213.7 0.1 copy.86
  213.8 0.1 rsqrt_multiply_fusion
  213.9 0.8 copy.89
  214.7 0.1 mul.205
  214.8 0.1 copy.85
  214.9 0.1 rsqrt_multiply_fusion.1
  215.0 0.8 copy.88
  215.8 40.4 %reduce-scatter.2.cloned.1.call-done = f32[256,128]{0,1:T(8,128)} async-done(((f32[16384,128]{0,1:T(8,128)}), f32[256,128]{0,1:T(8,128)}) %reduce-scatter.2.cloned.1.call-update) | async-done | bytes 131088 | tf_op jit(solution)/shard_map/reduce_scatter | solution.py:107
  256.2 1.1 fusion.12
  257.4 0.7 copy.87
  (34 shorter events, 0.1 us)
Async XLA Ops:
  7.2 13.4 %copy-start = (bf16[16,32,256]{2,1,0:T(8,128)(2,1)S(1)}, bf16[16,32,256]{2,1,0:T(8,128)(2,1)}, u32[]{:S(2)}) copy-start(bf16[16,32,256]{2,1,0:T(8,128)(2,1)} %param.17) | copy-start | bytes 786436
  7.2 94.1 %all-gather.2.cloned.1.call-start = ((), (), s32[]{:S(2)}) async-start(), calls=%async_computation.6 | async-start | bytes 8519680 | tf_op jit(solution)/shard_map/all_gather | solution.py:16
  9.7 246.5 %reduce-scatter.2.cloned.1.call-start = ((), (), s32[]{:S(2)}) async-start(), calls=%async_computation.7 | async-start | bytes 8519680 | tf_op jit(solution)/shard_map/reduce_scatter | solution.py:107
  19.9 0.7 copy-start.14
  19.9 0.9 copy-start.3
  22.2 95.2 %all-to-all-start.1 = ((f32[64,128,32]{1,2,0:T(8,128)}), f32[64,128,32]{1,2,0:T(8,128)S(1)}, u32[]{:S(2)}, u32[]{:S(2)}) async-start(f32[64,128,32]{1,2,0:T(8,128)} %broadcast_in_dim.23), calls=%async_computation.2 | async-start | bytes 2097152 | tf_op jit(solution)/shard_map/all_to_all | solution.py:28
  101.3 6.8 %copy-start.2 = (bf16[16384,129]{1,0:T(8,128)(2,1)S(1)}, bf16[16384,129]{1,0:T(8,128)(2,1)}, u32[]{:S(2)}) copy-start(bf16[16384,129]{1,0:T(8,128)(2,1)} %all-gather.2.cloned.1.call-done) | copy-start | bytes 12681220
  101.3 15.8 %copy-start.4 = (bf16[256,16,32]{0,2,1:T(8,128)(2,1)S(1)}, bf16[256,16,32]{0,2,1:T(8,128)(2,1)}, u32[]{:S(2)}) copy-start(bf16[256,16,32]{0,2,1:T(8,128)(2,1)} %param.16) | copy-start | bytes 786436
  115.1 2.0 copy-start.1
  117.1 63.4 %copy-start.13 = (s32[16]{0:T(128)S(1)}, s32[16]{0:T(128)}, u32[]{:S(2)}) copy-start(s32[16]{0:T(128)} %param.19) | copy-start | bytes 196
  118.5 74.2 %copy-start.9 = (f32[8,256]{1,0:T(8,128)S(1)}, f32[8,256]{1,0:T(8,128)}, u32[]{:S(2)}) copy-start(f32[8,256]{1,0:T(8,128)} %param.22) | copy-start | bytes 24580
  118.5 74.2 %copy-start.10 = (f32[8,256]{1,0:T(8,128)S(1)}, f32[8,256]{1,0:T(8,128)}, u32[]{:S(2)}) copy-start(f32[8,256]{1,0:T(8,128)} %param.25) | copy-start | bytes 24580
  118.5 35.5 %all-to-all-start = ((f32[64,128,32]{1,2,0:T(8,128)}), f32[64,128,32]{1,2,0:T(8,128)S(1)}, u32[]{:S(2)}, u32[]{:S(2)}) async-start(f32[64,128,32]{1,2,0:T(8,128)} %broadcast_in_dim.20), calls=%async_computation | async-start | bytes 2097152 | tf_op jit(solution)/shard_map/all_to_all | solution.py:28
  156.6 17.0 %all-to-all-start.2 = ((bf16[4,256,16,32]{1,3,2,0:T(8,128)(2,1)}), bf16[4,256,16,32]{1,3,2,0:T(8,128)(2,1)S(1)}, u32[]{:S(2)}, u32[]{:S(2)}) async-start(bf16[4,256,16,32]{1,3,2,0:T(8,128)(2,1)} %broadcast_in_dim.24), calls=%async_computation.3 | async-start | bytes 2097152 | tf_op jit(solution)/shard_map/all_to_all | solution.py:28
  174.8 17.0 %all-to-all-start.3 = ((bf16[4,16,32,256]{3,2,1,0:T(8,128)(2,1)}), bf16[4,16,32,256]{3,2,1,0:T(8,128)(2,1)S(1)}, u32[]{:S(2)}, u32[]{:S(2)}) async-start(bf16[4,16,32,256]{3,2,1,0:T(8,128)(2,1)} %broadcast_in_dim.25), calls=%async_computation.4 | async-start | bytes 2097152 | tf_op jit(solution)/shard_map/all_to_all | solution.py:28
  192.9 20.9 %copy-start.6 = (f32[8,256]{1,0:T(8,128)}, f32[8,256]{1,0:T(8,128)S(1)}, u32[]{:S(2)}) copy-start(f32[8,256]{1,0:T(8,128)S(1)} %get-tuple-element.80) | copy-start | bytes 24580
  192.9 22.0 %copy-start.5 = (f32[8,256]{1,0:T(8,128)}, f32[8,256]{1,0:T(8,128)S(1)}, u32[]{:S(2)}) copy-start(f32[8,256]{1,0:T(8,128)S(1)} %get-tuple-element.71) | copy-start | bytes 24580
  193.7 19.7 %all-to-all-start.4 = ((f32[64,1,520]{2,1,0:T(1,128)}), f32[64,1,520]{2,1,0:T(1,128)S(1)}, u32[]{:S(2)}, u32[]{:S(2)}) async-start(f32[64,1,520]{2,1,0:T(1,128)} %broadcast_in_dim.26), calls=%async_computation.5 | async-start | bytes 327680 | tf_op jit(solution)/shard_map/all_to_all | solution.py:28
  200.8 12.8 %copy-start.11 = (f32[8,32]{1,0:T(8,128)S(1)}, f32[8,32]{1,0:T(8,128)}, u32[]{:S(2)}) copy-start(f32[8,32]{1,0:T(8,128)} %param.24) | copy-start | bytes 3076
  200.8 14.0 %copy-start.12 = (f32[8,32]{1,0:T(8,128)S(1)}, f32[8,32]{1,0:T(8,128)}, u32[]{:S(2)}) copy-start(f32[8,32]{1,0:T(8,128)} %param.23) | copy-start | bytes 3076
  213.7 44.4 %copy-start.7 = (f32[8,32]{1,0:T(8,128)}, f32[8,32]{1,0:T(8,128)S(1)}, u32[]{:S(2)}) copy-start(f32[8,32]{1,0:T(8,128)S(1)} %get-tuple-element.69) | copy-start | bytes 3076
  214.8 43.3 %copy-start.8 = (f32[8,32]{1,0:T(8,128)}, f32[8,32]{1,0:T(8,128)S(1)}, u32[]{:S(2)}) copy-start(f32[8,32]{1,0:T(8,128)S(1)} %multiply_add_fusion.5) | copy-start | bytes 3076
Sparse Core Ops, SparseCore 0:
  11.4 89.9 all-gather.1
  105.5 150.6 reduce-scatter.1
where the time goes:
time: 266 us; the launch traced here: 265 us
  waiting for transfers between devices  164 us (62%)
  starting transfers between devices  36.1 us (14%)
  matrix products  21 us (8%)
  other arithmetic  15.7 us (6%)
  between operations  15 us (6%)
  local copies, waits for them, and re-layouts  13 us (5%)
    all_gather x1, waiting for transfers between devices, gather_turned(): filled = lax.all_gather(both, axis, axis=0, tiled=True)  67.1 us
    all_to_all x5, waiting for transfers between devices, copy_for_each(): return lax.all_to_all(copies, axis, split_axis=0, concat_axis=0, tiled=True)  56.6 us
    reduce_scatter x1, waiting for transfers between devices, on_device(): lax.psum_scatter(lax.dot_general(weight, output_gradient, contract_last,...  40.4 us
    all_to_all x5, starting transfers between devices, copy_for_each(): return lax.all_to_all(copies, axis, split_axis=0, concat_axis=0, tiled=True)  36 us
    dot_general x1, matrix products, on_device(): lax.dot_general(weight, output_gradient, contract_last, preferred_element...  9.48 us
    convert_element_type x1, other arithmetic, on_device(): (whole_f * scale * whole_gain.astype(jnp.float32)).astype(jnp.bfloat16)  6.95 us
    dot_general x1, matrix products, on_device(): jnp.dot(normed_full, weight, preferred_element_type=jnp.float32)  6.28 us
    unnamed x34, local copies, waits for them, and re-layouts  6.13 us
  transfers between devices with their start and end apart: 7, of which 6 were waited for; matrix products, arithmetic and copies ran while one was open for 16% of the time, Pallas kernels for 0%

commit v1 on v0

--- a/solution.py
+++ b/solution.py
@@ -13,7 +13,9 @@
     turned = [jnp.moveaxis(a, dim, 0) for a, dim in zip(arrays, dims)]
     widths = [t[0].size for t in turned]
     both = jnp.concatenate([t.reshape(-1, w) for t, w in zip(turned, widths)], axis=1)
-    filled = lax.all_gather(both, axis, axis=0, tiled=True)
+    filled = jnp.concatenate(
+        lax.all_to_all(jnp.stack([both] * lax.axis_size(axis)), axis, 0, 0), axis=0
+    )
     pieces = jnp.split(filled, [sum(widths[:k]) for k in range(1, len(widths))], axis=1)
     return tuple(
         (

time: 266 us -> 284 us (1.068)
  local copies, waits for them, and re-layouts: 13 us -> 23.7 us
  starting transfers between devices: 36.1 us -> 42.9 us
    all_to_all x0 -> x1, waiting for transfers between devices: none -> 93.5 us  [gather_turned(): lax.all_to_all(jnp.stack([both] * lax.axis_size(axis)), axis, 0, 0)]
    all_gather x1 -> x0, waiting for transfers between devices: 67.1 us -> none  [gather_turned(): filled = lax.all_gather(both, axis, axis=0, tiled=True)]
    reduce_scatter x1, waiting for transfers between devices: 40.4 us -> 0.01 us  [on_device(): lax.psum_scatter(lax.dot_general(weight, output_gradient, contract_last,...]
    all_to_all x0 -> x1, starting transfers between devices: none -> 12.3 us  [gather_turned(): lax.all_to_all(jnp.stack([both] * lax.axis_size(axis)), axis, 0, 0)]
    all_to_all x5, waiting for transfers between devices: 56.6 us -> 68.9 us  [copy_for_each(): return lax.all_to_all(copies, axis, split_axis=0, concat_axis=0, tiled=True)]
    all_to_all x0 -> x1, local copies, waits for them, and re-layouts: none -> 9.53 us  [gather_turned(): lax.all_to_all(jnp.stack([both] * lax.axis_size(axis)), axis, 0, 0)]
    all_to_all x5, starting transfers between devices: 36 us -> 30.5 us  [copy_for_each(): return lax.all_to_all(copies, axis, split_axis=0, concat_axis=0, tiled=True)]
    unnamed x34 -> x33, local copies, waits for them, and re-layouts: 6.13 us -> 4.97 us
  transfers between devices with their start and end apart: 7 -> 7, of which waited for: 6 -> 6; matrix products, arithmetic and copies ran while one was open for 16% -> 19% of each run, Pallas kernels for 0% -> 0%
where the time goes in v1:
time: 284 us; the launch traced here: 281 us
  waiting for transfers between devices  162 us (57%)
  starting transfers between devices  42.9 us (15%)
  local copies, waits for them, and re-layouts  23.7 us (8%)
  matrix products  20.9 us (7%)
  other arithmetic  15.8 us (6%)
  between operations  14.9 us (5%)
    all_to_all x1, waiting for transfers between devices, gather_turned(): lax.all_to_all(jnp.stack([both] * lax.axis_size(axis)), axis, 0, 0)  93.5 us
    all_to_all x5, waiting for transfers between devices, copy_for_each(): return lax.all_to_all(copies, axis, split_axis=0, concat_axis=0, tiled=True)  68.9 us
    all_to_all x5, starting transfers between devices, copy_for_each(): return lax.all_to_all(copies, axis, split_axis=0, concat_axis=0, tiled=True)  30.5 us
    all_to_all x1, starting transfers between devices, gather_turned(): lax.all_to_all(jnp.stack([both] * lax.axis_size(axis)), axis, 0, 0)  12.3 us
    all_to_all x1, local copies, waits for them, and re-layouts, gather_turned(): lax.all_to_all(jnp.stack([both] * lax.axis_size(axis)), axis, 0, 0)  9.53 us
    dot_general x1, matrix products, on_device(): lax.dot_general(weight, output_gradient, contract_last, preferred_element...  9.44 us
    convert_element_type x1, other arithmetic, on_device(): (whole_f * scale * whole_gain.astype(jnp.float32)).astype(jnp.bfloat16)  6.95 us
    dot_general x1, matrix products, on_device(): jnp.dot(normed_full, weight, preferred_element_type=jnp.float32)  6.19 us
  transfers between devices with their start and end apart: 7, of which 6 were waited for; matrix products, arithmetic and copies ran while one was open for 19% of the time, Pallas kernels for 0%

profile of v1, /device:TPU:6, one launch (start us, length us, event | category | flops | bytes accessed | tf_op | source)
XLA Modules:
  0.0 280.6 jit_solution(1399471838292364018)
XLA Ops:
  7.2 0.0 copy-start
  7.2 0.7 reshape.140
  7.9 0.8 pad_maximum_fusion
  8.8 2.3 stack.2
  11.1 12.3 %all-to-all-start = ((bf16[64,256,129]{1,2,0:T(8,128)(2,1)}), bf16[64,256,129]{1,2,0:T(8,128)(2,1)}, u32[]{:S(2)}, u32[]{:S(2)}) async-start(bf16[64,256,129]{1,2,0:T(8,128)(2,1)} %stack.2), calls=%async_computation | async-start | bytes 8912896 | tf_op jit(solution)/shard_map/all_to_all | solution.py:17
  23.4 0.0 reduce-scatter.2.cloned.1.call-start
  24.2 9.4 %convolution_bitcast_fusion = f32[16384,128]{0,1:T(8,128)} fusion(bf16[16384,256]{1,0:T(8,128)(2,1)} %param.15, bf16[128,256]{1,0:T(8,128)(2,1)S(1)} %copy-done.3, pred[128]{0:T(512)(128)(4,1)S(1)} %iota_compare_fusion.1), kind=kOutput, calls=%fused_computation | convolution fusion | flops 1073774592 | bytes 16842880 | tf_op jit(solution)/shard_map/dot_general | solution.py:110
  33.6 0.0 reduce-scatter.2.cloned.1.call-update
  33.6 0.6 copy-done.14
  34.3 0.3 fusion.6
  34.6 93.5 %all-to-all-done = bf16[64,256,129]{1,2,0:T(8,128)(2,1)} async-done(((bf16[64,256,129]{1,2,0:T(8,128)(2,1)}), bf16[64,256,129]{1,2,0:T(8,128)(2,1)}, u32[]{:S(2)}, u32[]{:S(2)}) %all-to-all-start) | async-done | bytes 4227104 | tf_op jit(solution)/shard_map/all_to_all | solution.py:17
  128.1 1.1 broadcast_in_dim.23
  129.2 6.1 %all-to-all-start.2 = ((f32[64,128,32]{1,2,0:T(8,128)}), f32[64,128,32]{1,2,0:T(8,128)S(1)}, u32[]{:S(2)}, u32[]{:S(2)}) async-start(f32[64,128,32]{1,2,0:T(8,128)} %broadcast_in_dim.23), calls=%async_computation.3 | async-start | bytes 2097152 | tf_op jit(solution)/shard_map/all_to_all | solution.py:30
  135.3 9.5 %copy.72 = bf16[64,256,129]{2,1,0:T(8,128)(2,1)} copy(bf16[64,256,129]{1,2,0:T(8,128)(2,1)} %all-to-all-done) | data formatting | bytes 8454144 | tf_op jit(solution)/shard_map/all_to_all | solution.py:17
  144.9 3.9 %fusion = f32[128]{0:T(128)S(1)} fusion(bf16[16384,129]{1,0:T(8,128)(2,1)} %bitcast.64), kind=kLoop, calls=%fused_computation.3 | loop fusion | flops 6291328 | bytes 4194816 | tf_op jit(solution)/shard_map/reduce_sum | solution.py:75
  148.8 2.9 %convert_reduce_fusion = f32[16384]{0:T(1024)S(1)} fusion(bf16[16384,129]{1,0:T(8,128)(2,1)} %bitcast.65), kind=kLoop, calls=%fused_computation.6 | loop fusion | flops 16384 | bytes 98304 | tf_op jit(solution)/shard_map/convert_element_type | solution.py:77
  151.7 6.9 %fusion.2 = bf16[16384,128]{1,0:T(8,128)(2,1)S(1)} fusion(f32[16384]{0:T(1024)S(1)} %convert_reduce_fusion, f32[128]{0:T(128)S(1)} %add_rsqrt_fusion, bf16[16384,129]{1,0:T(8,128)(2,1)S(1)} %bitcast.66), kind=kLoop, calls=%fused_computation.5 | loop fusion | flops 8388608 | bytes 8454656 | tf_op jit(solution)/shard_map/convert_element_type | solution.py:77
  158.7 2.0 copy-done.2
  160.7 0.2 fusion.5
  160.9 8.8 %all-to-all-done.2 = f32[64,128,32]{1,2,0:T(8,128)S(1)} async-done(((f32[64,128,32]{1,2,0:T(8,128)}), f32[64,128,32]{1,2,0:T(8,128)S(1)}, u32[]{:S(2)}, u32[]{:S(2)}) %all-to-all-start.2) | async-done | bytes 1048608 | tf_op jit(solution)/shard_map/all_to_all | solution.py:30
  169.7 1.2 broadcast_in_dim.20
  170.9 7.6 %all-to-all-start.1 = ((f32[64,128,32]{1,2,0:T(8,128)}), f32[64,128,32]{1,2,0:T(8,128)S(1)}, u32[]{:S(2)}, u32[]{:S(2)}) async-start(f32[64,128,32]{1,2,0:T(8,128)} %broadcast_in_dim.20), calls=%async_computation.1 | async-start | bytes 2097152 | tf_op jit(solution)/shard_map/all_to_all | solution.py:30
  178.5 0.1 reduce_sum.130
  178.6 32.9 %all-to-all-done.1 = f32[64,128,32]{1,2,0:T(8,128)S(1)} async-done(((f32[64,128,32]{1,2,0:T(8,128)}), f32[64,128,32]{1,2,0:T(8,128)S(1)}, u32[]{:S(2)}, u32[]{:S(2)}) %all-to-all-start.1) | async-done | bytes 1048608 | tf_op jit(solution)/shard_map/all_to_all | solution.py:30
  211.5 0.1 reduce_sum.128
  211.7 0.3 fusion.4
  211.9 1.2 broadcast_in_dim.25
  213.1 4.7 %all-to-all-start.4 = ((bf16[4,16,32,256]{3,2,1,0:T(8,128)(2,1)}), bf16[4,16,32,256]{3,2,1,0:T(8,128)(2,1)S(1)}, u32[]{:S(2)}, u32[]{:S(2)}) async-start(bf16[4,16,32,256]{3,2,1,0:T(8,128)(2,1)} %broadcast_in_dim.25), calls=%async_computation.5 | async-start | bytes 2097152 | tf_op jit(solution)/shard_map/all_to_all | solution.py:30
  217.8 1.1 fusion.3
  218.9 0.1 copy.73
  219.0 11.7 %all-to-all-done.4 = bf16[4,16,32,256]{3,2,1,0:T(8,128)(2,1)S(1)} async-done(((bf16[4,16,32,256]{3,2,1,0:T(8,128)(2,1)}), bf16[4,16,32,256]{3,2,1,0:T(8,128)(2,1)S(1)}, u32[]{:S(2)}, u32[]{:S(2)}) %all-to-all-start.4) | async-done | bytes 1048608 | tf_op jit(solution)/shard_map/all_to_all | solution.py:30
  230.7 1.2 broadcast_in_dim.24
  231.9 5.6 %all-to-all-start.3 = ((bf16[4,256,16,32]{1,3,2,0:T(8,128)(2,1)}), bf16[4,256,16,32]{1,3,2,0:T(8,128)(2,1)S(1)}, u32[]{:S(2)}, u32[]{:S(2)}) async-start(bf16[4,256,16,32]{1,3,2,0:T(8,128)(2,1)} %broadcast_in_dim.24), calls=%async_computation.4 | async-start | bytes 2097152 | tf_op jit(solution)/shard_map/all_to_all | solution.py:30
  237.5 0.2 convert_reduce_fusion.1
  237.7 0.7 fusion.21
  238.4 0.1 copy.77
  238.4 0.1 reshape.144
  238.5 10.9 %all-to-all-done.3 = bf16[4,256,16,32]{1,3,2,0:T(8,128)(2,1)S(1)} async-done(((bf16[4,256,16,32]{1,3,2,0:T(8,128)(2,1)}), bf16[4,256,16,32]{1,3,2,0:T(8,128)(2,1)S(1)}, u32[]{:S(2)}, u32[]{:S(2)}) %all-to-all-start.3) | async-done | bytes 1048608 | tf_op jit(solution)/shard_map/all_to_all | solution.py:30
  249.4 0.2 convert_reduce_fusion.2
  249.6 0.7 fusion.19
  250.3 0.1 copy.75
  250.4 0.1 reshape.143
  250.5 0.1 fusion.40
  250.6 0.0 copy-start.5
  250.6 0.0 copy-start.6
  250.6 0.8 broadcast_in_dim.26
  251.4 6.5 %all-to-all-start.5 = ((f32[64,1,520]{2,1,0:T(1,128)}), f32[64,1,520]{2,1,0:T(1,128)S(1)}, u32[]{:S(2)}, u32[]{:S(2)}) async-start(f32[64,1,520]{2,1,0:T(1,128)} %broadcast_in_dim.26), calls=%async_computation.6 | async-start | bytes 327680 | tf_op jit(solution)/shard_map/all_to_all | solution.py:30
  257.9 0.0 copy-start.11
  257.9 0.0 copy-start.12
  257.9 6.2 %fusion.41 = f32[128,256]{1,0:T(8,128)S(1)} fusion(bf16[16384,128]{1,0:T(8,128)(2,1)} %copy-done.2, bf16[16384,256]{1,0:T(8,128)(2,1)} %param.15), kind=kOutput, calls=%fused_computation.74 | convolution fusion | flops 1073741824 | bytes 12713984 | tf_op jit(solution)/shard_map/dot_general | solution.py:78
  264.1 0.9 fusion.13
  264.9 4.5 %all-to-all-done.5 = f32[64,1,520]{2,1,0:T(1,128)S(1)} async-done(((f32[64,1,520]{2,1,0:T(1,128)}), f32[64,1,520]{2,1,0:T(1,128)S(1)}, u32[]{:S(2)}, u32[]{:S(2)}) %all-to-all-start.5) | async-done | bytes 133152 | tf_op jit(solution)/shard_map/all_to_all | solution.py:30
  269.5 0.1 reduce_sum.137
  269.6 0.1 mul.205
  269.7 0.1 copy.79
  269.8 0.1 rsqrt_multiply_fusion.1
  269.9 0.8 copy.82
  270.7 0.1 mul.211
  270.8 0.1 fusion.39
  270.9 0.1 copy.80
  271.0 0.1 rsqrt_multiply_fusion
  271.1 0.8 copy.83
  271.9 1.1 fusion.12
  273.0 0.7 copy.81
  (34 shorter events, 0.1 us)
Async XLA Ops:
  7.2 27.1 %copy-start = (bf16[16,32,256]{2,1,0:T(8,128)(2,1)S(1)}, bf16[16,32,256]{2,1,0:T(8,128)(2,1)}, u32[]{:S(2)}) copy-start(bf16[16,32,256]{2,1,0:T(8,128)(2,1)} %param.17) | copy-start | bytes 786436
  7.2 17.0 %copy-start.3 = (bf16[128,256]{1,0:T(8,128)(2,1)S(1)}, bf16[128,256]{1,0:T(8,128)(2,1)}, u32[]{:S(2)}) copy-start(bf16[128,256]{1,0:T(8,128)(2,1)} %param.21) | copy-start | bytes 196612
  11.1 117.0 %all-to-all-start = ((bf16[64,256,129]{1,2,0:T(8,128)(2,1)}), bf16[64,256,129]{1,2,0:T(8,128)(2,1)}, u32[]{:S(2)}, u32[]{:S(2)}) async-start(bf16[64,256,129]{1,2,0:T(8,128)(2,1)} %stack.2), calls=%async_computation | async-start | bytes 8912896 | tf_op jit(solution)/shard_map/all_to_all | solution.py:17
  23.4 248.5 %reduce-scatter.2.cloned.1.call-start = ((), (), s32[]{:S(2)}) async-start(), calls=%async_computation.7 | async-start | bytes 8519680 | tf_op jit(solution)/shard_map/reduce_scatter | solution.py:109
  33.6 0.7 copy-start.14
  129.2 40.5 %all-to-all-start.2 = ((f32[64,128,32]{1,2,0:T(8,128)}), f32[64,128,32]{1,2,0:T(8,128)S(1)}, u32[]{:S(2)}, u32[]{:S(2)}) async-start(f32[64,128,32]{1,2,0:T(8,128)} %broadcast_in_dim.23), calls=%async_computation.3 | async-start | bytes 2097152 | tf_op jit(solution)/shard_map/all_to_all | solution.py:30
  144.9 6.8 %copy-start.1 = (bf16[64,256,129]{2,1,0:T(8,128)(2,1)S(1)}, bf16[64,256,129]{2,1,0:T(8,128)(2,1)}, u32[]{:S(2)}) copy-start(bf16[64,256,129]{2,1,0:T(8,128)(2,1)} %copy.72) | copy-start | bytes 12681220
  144.9 15.8 %copy-start.4 = (bf16[256,16,32]{0,2,1:T(8,128)(2,1)S(1)}, bf16[256,16,32]{0,2,1:T(8,128)(2,1)}, u32[]{:S(2)}) copy-start(bf16[256,16,32]{0,2,1:T(8,128)(2,1)} %param.16) | copy-start | bytes 786436
  158.7 2.0 copy-start.2
  160.7 77.0 %copy-start.13 = (s32[16]{0:T(128)S(1)}, s32[16]{0:T(128)}, u32[]{:S(2)}) copy-start(s32[16]{0:T(128)} %param.19) | copy-start | bytes 196
  170.9 79.6 %copy-start.9 = (f32[8,256]{1,0:T(8,128)S(1)}, f32[8,256]{1,0:T(8,128)}, u32[]{:S(2)}) copy-start(f32[8,256]{1,0:T(8,128)} %param.22) | copy-start | bytes 24580
  170.9 79.6 %copy-start.10 = (f32[8,256]{1,0:T(8,128)S(1)}, f32[8,256]{1,0:T(8,128)}, u32[]{:S(2)}) copy-start(f32[8,256]{1,0:T(8,128)} %param.25) | copy-start | bytes 24580
  170.9 40.6 %all-to-all-start.1 = ((f32[64,128,32]{1,2,0:T(8,128)}), f32[64,128,32]{1,2,0:T(8,128)S(1)}, u32[]{:S(2)}, u32[]{:S(2)}) async-start(f32[64,128,32]{1,2,0:T(8,128)} %broadcast_in_dim.20), calls=%async_computation.1 | async-start | bytes 2097152 | tf_op jit(solution)/shard_map/all_to_all | solution.py:30
  213.1 17.6 %all-to-all-start.4 = ((bf16[4,16,32,256]{3,2,1,0:T(8,128)(2,1)}), bf16[4,16,32,256]{3,2,1,0:T(8,128)(2,1)S(1)}, u32[]{:S(2)}, u32[]{:S(2)}) async-start(bf16[4,16,32,256]{3,2,1,0:T(8,128)(2,1)} %broadcast_in_dim.25), calls=%async_computation.5 | async-start | bytes 2097152 | tf_op jit(solution)/shard_map/all_to_all | solution.py:30
  231.9 17.5 %all-to-all-start.3 = ((bf16[4,256,16,32]{1,3,2,0:T(8,128)(2,1)}), bf16[4,256,16,32]{1,3,2,0:T(8,128)(2,1)S(1)}, u32[]{:S(2)}, u32[]{:S(2)}) async-start(bf16[4,256,16,32]{1,3,2,0:T(8,128)(2,1)} %broadcast_in_dim.24), calls=%async_computation.4 | async-start | bytes 2097152 | tf_op jit(solution)/shard_map/all_to_all | solution.py:30
  250.6 19.2 %copy-start.5 = (f32[8,256]{1,0:T(8,128)}, f32[8,256]{1,0:T(8,128)S(1)}, u32[]{:S(2)}) copy-start(f32[8,256]{1,0:T(8,128)S(1)} %get-tuple-element.71) | copy-start | bytes 24580
  250.6 20.4 %copy-start.6 = (f32[8,256]{1,0:T(8,128)}, f32[8,256]{1,0:T(8,128)S(1)}, u32[]{:S(2)}) copy-start(f32[8,256]{1,0:T(8,128)S(1)} %get-tuple-element.80) | copy-start | bytes 24580
  251.4 18.1 %all-to-all-start.5 = ((f32[64,1,520]{2,1,0:T(1,128)}), f32[64,1,520]{2,1,0:T(1,128)S(1)}, u32[]{:S(2)}, u32[]{:S(2)}) async-start(f32[64,1,520]{2,1,0:T(1,128)} %broadcast_in_dim.26), calls=%async_computation.6 | async-start | bytes 327680 | tf_op jit(solution)/shard_map/all_to_all | solution.py:30
  257.9 11.8 %copy-start.11 = (f32[8,32]{1,0:T(8,128)S(1)}, f32[8,32]{1,0:T(8,128)}, u32[]{:S(2)}) copy-start(f32[8,32]{1,0:T(8,128)} %param.23) | copy-start | bytes 3076
  257.9 12.9 %copy-start.12 = (f32[8,32]{1,0:T(8,128)S(1)}, f32[8,32]{1,0:T(8,128)}, u32[]{:S(2)}) copy-start(f32[8,32]{1,0:T(8,128)} %param.24) | copy-start | bytes 3076
  269.7 4.1 %copy-start.7 = (f32[8,32]{1,0:T(8,128)}, f32[8,32]{1,0:T(8,128)S(1)}, u32[]{:S(2)}) copy-start(f32[8,32]{1,0:T(8,128)S(1)} %multiply_add_fusion.5) | copy-start | bytes 3076
  270.9 2.9 %copy-start.8 = (f32[8,32]{1,0:T(8,128)}, f32[8,32]{1,0:T(8,128)S(1)}, u32[]{:S(2)}) copy-start(f32[8,32]{1,0:T(8,128)S(1)} %get-tuple-element.69) | copy-start | bytes 3076
Sparse Core Ops, SparseCore 0:
  33.7 177.2 reduce-scatter.1
